TPU v7x, 32 devices: a whole 2x2x4 slice. The times are simulated.
32 devices in a mesh: side: 2 (over x), grp: 4 (over z), blk: 4 (over y, core).
Axes of the slice: x: 2, y: 2, z: 4, core: 2. Of those that a mesh axis runs over, the one named last changes fastest.
Arguments:
- embed_codes: bfloat16 [2, 8192, 128], P('side', ('grp', 'blk')), may hold values from -4 to 4
- embed_exps: int32 [2, 64], P('side', ('grp', 'blk')), may hold values from -1 to 1
- degrees: int32 [2, 8192], P('side', ('grp', 'blk')), may hold values from 16 to 128
- adjacency: bfloat16 [2, 1536, 128, 128], P('side', ('grp', 'blk')), may hold values from 0 to 1
- block_index: int32 [2, 2, 1536], P('side', None, ('grp', 'blk')), may hold values from 0 to 16, as said below
Outputs:
- layer_rows: bfloat16 [2, 8192, 128], P('side', ('grp', 'blk'))
Inputs may be any that keep to these rules, and one draw needn't show every extreme that they name: `block_index`: each device's list of 96 slots: its used slots come first, in non-decreasing source tile (row 1 below 16), with distinct (destination, source) pairs and destination tiles below 16; the remaining slots have source 16 and destination 0. Every list uses 96 // 4 slots or more, and in each section one list uses all 96.
All inputs are finite; a program needn't handle non-finite values.
Results may differ from a plain program's by a relative error of at most 0.0048.
Values may be sent and summed in bfloat16 or wider, within the bound.
No kernel may reach another device: no remote copies, remote signals or barrier semaphores. Data moves between devices by JAX's collectives and lax.ppermute only.
A program may use at most 128 MiB of HBM per device.

v0:
```python
import functools

import jax
import jax.numpy as jnp
from jax import lax
from jax.experimental import pallas as pl
from jax.experimental.pallas import tpu as pltpu
from jax.sharding import PartitionSpec as P

UNROLL = 8
STAGES = 4
VMEM = pl.BlockSpec(memory_space=pltpu.VMEM)
SMEM = pl.BlockSpec(memory_space=pltpu.SMEM)
HBM = pl.BlockSpec(memory_space=pltpu.HBM)
LIMIT = pltpu.CompilerParams(vmem_limit_bytes=48 * 1024 * 1024)


def in_hbm(*arrays):
    return [pltpu.with_memory_space_constraint(array, pltpu.HBM) for array in arrays]


def split(value, size):
    if size & (size - 1) == 0:
        return value >> (size.bit_length() - 1), value & (size - 1)
    return value // size, value % size


def scale_kernel(exps_hbm, degrees_hbm, codes_hbm, rows, exps_ref, degrees, codes, sems):
    pairs = [(exps_hbm, exps_ref), (degrees_hbm, degrees), (codes_hbm, codes)]
    fetches = [
        pltpu.make_async_copy(held, wanted, sems.at[at])
        for at, (held, wanted) in enumerate(pairs)
    ]
    for fetch in fetches:
        fetch.start()
    fetches[0].wait()
    fetches[1].wait()
    tiles_dev, tile_rows, row_width = rows.shape
    inverse = lax.rsqrt(degrees[...].astype(jnp.float32))
    factors = []
    for tile in range(tiles_dev):
        lanes = inverse[:, tile * tile_rows : (tile + 1) * tile_rows]
        scale = jnp.exp2(jnp.full(lanes.shape, exps_ref[0, tile], jnp.int32).astype(jnp.float32))
        factors.append(jnp.broadcast_to(lanes * scale, (row_width, tile_rows)).T)
    fetches[2].wait()
    for tile, factor in enumerate(factors):
        rows[tile] = (codes[tile].astype(jnp.float32) * factor).astype(rows.dtype)


def scale_rows(codes, exps, degrees):
    return pl.pallas_call(
        scale_kernel,
        out_shape=jax.ShapeDtypeStruct(codes.shape, jnp.bfloat16),
        in_specs=[HBM] * 3,
        out_specs=VMEM,
        scratch_shapes=[
            pltpu.SMEM(exps.shape, exps.dtype),
            pltpu.VMEM(degrees.shape, degrees.dtype),
            pltpu.VMEM(codes.shape, codes.dtype),
            pltpu.SemaphoreType.DMA((3,)),
        ],
        compiler_params=LIMIT,
        cost_estimate=pl.CostEstimate(
            flops=codes.size, bytes_accessed=4 * codes.size, transcendentals=0
        ),
    )(*in_hbm(exps, degrees, codes))


def stage_kernel(
    blks, groups, tiles_dev, place_ref, index_hbm, blocks_hbm, order_ref, blocks, index_ref, sems
):
    fetch = pltpu.make_async_copy(index_hbm, index_ref, sems.at[0])
    fetch.start()
    copy = pltpu.make_async_copy(blocks_hbm, blocks, sems.at[1])
    copy.start()
    fetch.wait()
    my_blk = place_ref[0]
    my_grp = place_ref[1]
    capacity = index_ref.shape[1]
    source_tiles = blks * tiles_dev

    def enlist(slot, nexts):
        target = index_ref[0, slot]
        origin = index_ref[1, slot]
        hop, row = split(origin, tiles_dev)
        chunk, tile = split(target, tiles_dev)
        hop = hop ^ my_blk
        chunk = chunk ^ my_grp
        near = jnp.where((chunk >= 2) & ((chunk & 1) == 1), 2, 3)
        stage = jnp.where((hop & 1) == 1, near, jnp.where(hop == 0, 0, 1))
        stage = jnp.where(origin < source_tiles, stage, STAGES)
        panel = (hop >> 1) - (stage == 1).astype(jnp.int32)
        word = pack(slot, panel * tiles_dev + row, chunk * tiles_dev + tile)
        where = jnp.int32(0)
        for at, position in enumerate(nexts):
            where = jnp.where(stage == at, position, where)
        order_ref[stage, where] = word
        return tuple(
            position + (stage == at).astype(jnp.int32) for at, position in enumerate(nexts)
        )

    ends = lax.fori_loop(0, capacity, enlist, (jnp.int32(0),) * STAGES, unroll=8)
    spare = pack(0, 0, groups * tiles_dev)
    for at, end in enumerate(ends):
        for extra in range(UNROLL):
            order_ref[at, end + extra] = spare
        order_ref[at, capacity + UNROLL] = split(end + (UNROLL - 1), UNROLL)[0]
    copy.wait()


def pack(slot, row, target):
    return (slot << 16) | (row << 8) | target


def unpack(word):
    return word >> 16, (word >> 8) & 255, word & 255


def stage_blocks(index, place, blocks, blks, groups, tiles_dev):
    capacity = blocks.shape[0]
    assert blks * tiles_dev < 256 and groups * tiles_dev < 256 and capacity < 2**15
    return pl.pallas_call(
        functools.partial(stage_kernel, blks, groups, tiles_dev),
        out_shape=[
            jax.ShapeDtypeStruct((STAGES + 1, capacity + 2 * UNROLL), jnp.int32),
            jax.ShapeDtypeStruct(blocks.shape, blocks.dtype),
        ],
        in_specs=[SMEM, HBM, HBM],
        out_specs=[SMEM, VMEM],
        scratch_shapes=[
            pltpu.SMEM(index.shape, index.dtype),
            pltpu.SemaphoreType.DMA((2,)),
        ],
        compiler_params=LIMIT,
        cost_estimate=pl.CostEstimate(flops=0, bytes_accessed=0, transcendentals=0),
    )(place, *in_hbm(index, blocks))


def add_products(stage, order_ref, blocks, source, total):
    @pl.loop(0, order_ref[stage, order_ref.shape[1] - UNROLL])
    def _(batch):
        made = []
        for part in range(UNROLL):
            slot, row, target = unpack(order_ref[stage, batch * UNROLL + part])
            product = jnp.dot(blocks[slot], source[row], preferred_element_type=jnp.float32)
            made.append((target, product))
        for target, product in made:
            total[target] += product


def gather_panels(panels, source):
    for at, panel in enumerate(panels):
        rows = panel.shape[0]
        source[at * rows : (at + 1) * rows] = panel[...]


def first_kernel(order_ref, panel, blocks, total):
    total[...] = jnp.zeros_like(total)
    add_products(0, order_ref, blocks, panel, total)


def second_kernel(order_ref, *refs):
    *panels, blocks, _, total, source = refs
    gather_panels(panels, source)
    add_products(1, order_ref, blocks, source, total)


def far_kernel(tiles_dev, chunks, order_ref, *refs):
    *panels, blocks, _, far, total, source = refs
    gather_panels(panels, source)
    add_products(2, order_ref, blocks, source, total)
    for at, chunk in enumerate(chunks):
        far[at] = total[chunk * tiles_dev : (chunk + 1) * tiles_dev].astype(far.dtype)


def near_kernel(tiles_dev, chunks, order_ref, *refs):
    *panels, blocks, total, own, near, mine, source = refs
    gather_panels(panels, source)
    add_products(3, order_ref, blocks, source, total)
    own[...] = total[:tiles_dev]
    near[...] = total[tiles_dev : 2 * tiles_dev].astype(near.dtype)
    for at, chunk in enumerate(chunks):
        mine[at] = total[chunk * tiles_dev : (chunk + 1) * tiles_dev]


def cost_of(slots, tile_rows, row_width):
    return pl.CostEstimate(
        flops=2 * slots * tile_rows * tile_rows * row_width,
        bytes_accessed=2 * slots * tile_rows * tile_rows,
        transcendentals=0,
    )


def shards(embed_codes, embed_exps, degrees, adjacency, block_index):
    tile_rows = adjacency.shape[2]
    row_width = embed_codes.shape[2]
    row_count = embed_codes.shape[1]
    capacity = adjacency.shape[1]
    tiles_dev = row_count // tile_rows
    groups = lax.axis_size("grp")
    blks = lax.axis_size("blk")
    part = (tiles_dev, tile_rows, row_width)
    dest_tiles = groups * tiles_dev
    source = scale_rows(embed_codes.reshape(part), embed_exps, degrees)

    def across(value, hop):
        pairs = [
            (side * blks + at, (1 - side) * blks + (at ^ hop))
            for side in range(2)
            for at in range(blks)
        ]
        return lax.ppermute(value, ("side", "blk"), pairs)

    def paired(value, axis, hop):
        return lax.ppermute(value, axis, [(at, at ^ hop) for at in range(lax.axis_size(axis))])

    place = jnp.stack([lax.axis_index("blk"), lax.axis_index("grp")]).astype(jnp.int32)
    straight, *diagonal = [across(source, hop) for hop in range(0, blks, 2)]
    order, blocks = stage_blocks(block_index[0], place, adjacency[0], blks, groups, tiles_dev)
    straight, order = lax.optimization_barrier((straight, order))
    total_shape = jax.ShapeDtypeStruct((dest_tiles + 1, tile_rows, row_width), jnp.float32)
    total = pl.pallas_call(
        first_kernel,
        out_shape=total_shape,
        in_specs=[SMEM] + [VMEM] * 2,
        out_specs=VMEM,
        compiler_params=LIMIT,
        cost_estimate=cost_of(capacity // 4, tile_rows, row_width),
    )(order, straight, blocks)
    *diagonal, total = lax.optimization_barrier((*diagonal, total))
    others = [paired(panel, "blk", 1) for panel in (straight, *diagonal)]
    total = pl.pallas_call(
        second_kernel,
        out_shape=total_shape,
        in_specs=[SMEM] + [VMEM] * (len(diagonal) + 2),
        out_specs=VMEM,
        input_output_aliases={len(diagonal) + 2: 0},
        scratch_shapes=[
            pltpu.VMEM((len(diagonal) * tiles_dev, tile_rows, row_width), jnp.bfloat16)
        ],
        compiler_params=LIMIT,
        cost_estimate=cost_of(capacity // 4, tile_rows, row_width),
    )(order, *diagonal, blocks, total)
    *others, total = lax.optimization_barrier((*others, total))
    others_scratch = [pltpu.VMEM((len(others) * tiles_dev, tile_rows, row_width), jnp.bfloat16)]
    far_chunks = range(3, groups, 2)
    far, total = pl.pallas_call(
        functools.partial(far_kernel, tiles_dev, far_chunks),
        out_shape=[
            jax.ShapeDtypeStruct((len(far_chunks),) + part, jnp.bfloat16),
            total_shape,
        ],
        in_specs=[SMEM] + [VMEM] * (len(others) + 2),
        out_specs=[VMEM, VMEM],
        input_output_aliases={len(others) + 2: 1},
        scratch_shapes=others_scratch,
        compiler_params=LIMIT,
        cost_estimate=cost_of(capacity // 8, tile_rows, row_width),
    )(order, *others, blocks, total)
    far_arrived = paired(far, "grp", 1)
    mine_chunks = range(2, groups, 2)
    own, near, mine = pl.pallas_call(
        functools.partial(near_kernel, tiles_dev, mine_chunks),
        out_shape=[
            jax.ShapeDtypeStruct(part, jnp.float32),
            jax.ShapeDtypeStruct(part, jnp.bfloat16),
            jax.ShapeDtypeStruct((len(mine_chunks),) + part, jnp.float32),
        ],
        in_specs=[SMEM] + [VMEM] * (len(others) + 2),
        out_specs=[VMEM] * 3,
        scratch_shapes=others_scratch,
        compiler_params=LIMIT,
        cost_estimate=cost_of(capacity // 2, tile_rows, row_width),
    )(order, *others, blocks, total)
    summed = own
    for at, hop in enumerate(mine_chunks):
        pair = (mine[at] + far_arrived[at].astype(jnp.float32)).astype(jnp.bfloat16)
        near, pair = lax.optimization_barrier((near, pair))
        summed = summed + paired(pair, "grp", hop).astype(jnp.float32)
    summed = summed + paired(near, "grp", 1).astype(jnp.float32)
    inverse = lax.rsqrt(degrees.astype(jnp.float32))
    return (summed.reshape(1, row_count, row_width) * inverse[..., None]).astype(jnp.bfloat16)


def solution(mesh):
    placed = (
        P("side", ("grp", "blk"), None),
        P("side", ("grp", "blk")),
        P("side", ("grp", "blk")),
        P("side", ("grp", "blk"), None, None),
        P("side", None, ("grp", "blk")),
    )
    return jax.shard_map(
        shards,
        mesh=mesh,
        in_specs=placed,
        out_specs=P("side", ("grp", "blk"), None),
        check_vma=False,
    )
```

profile of v0, /device:TPU:0, one launch (start us, length us, event | category | flops | bytes accessed | tf_op | source)
XLA Modules:
  0.0 31.0 jit_solution(3156441567701568223)
XLA Ops:
  0.0 1.0 %shard_map.55 = bf16[4,128,128]{2,1,0:T(8,128)(2,1)S(1)} custom-call(s32[1,4]{1,0:T(1,128)} %exps_hbm.1, s32[1,512]{1,0:T(1,128)} %degrees_hbm.1, bf16[4,128,128]{2,1,0:T(8,128)(2,1)} %bitcast.15), custom_call_target="tpu_custom_call" | custom-call | flops 65536 | bytes 262144 | tf_op jit(solution)/shard_map/pallas_call | solution.py:51
  1.0 3.0 %collective-permute-start = (bf16[4,128,128]{2,1,0:T(8,128)(2,1)S(1)}, bf16[4,128,128]{2,1,0:T(8,128)(2,1)S(1)}, u32[]{:S(2)}, u32[]{:S(2)}) collective-permute-start(bf16[4,128,128]{2,1,0:T(8,128)(2,1)S(1)} %shard_map.55), channel_id=1, source_target_pairs={{0,16},{1,17},{2,18},{3,19},{16,0},{17,1},{18,2},{19,3},{4,20},{5,... | collective-permute-start | bytes 393224 | tf_op jit(solution)/shard_map/ppermute | solution.py:212
  4.0 1.5 %collective-permute-start.2 = (bf16[4,128,128]{2,1,0:T(8,128)(2,1)S(1)}, bf16[4,128,128]{2,1,0:T(8,128)(2,1)S(1)}, u32[]{:S(2)}, u32[]{:S(2)}) collective-permute-start(bf16[4,128,128]{2,1,0:T(8,128)(2,1)S(1)} %shard_map.55), channel_id=1, source_target_pairs={{0,18},{1,19},{2,16},{3,17},{16,2},{17,3},{18,0},{19,1},{4,22},{5,... | collective-permute-start | bytes 393224 | tf_op jit(solution)/shard_map/ppermute | solution.py:212
  5.5 0.1 pad_add_fusion.place_ref
  5.5 3.8 %shard_map.56 = (s32[5,112]{1,0:T(8,128)S(1)}, bf16[96,128,128]{2,1,0:T(8,128)(2,1)S(1)}) custom-call(s32[2]{0:T(128)S(1)} %pad_add_fusion.place_ref, s32[2,96]{1,0:T(2,128)} %bitcast.17, bf16[96,128,128]{2,1,0:T(8,128)(2,1)} %bitcast.13), custom_call_target="tpu_custom_call" | custom-call | tf_op jit(solution)/shard_map/pallas_call | solution.py:122
  9.3 0.0 collective-permute-done.panel
  9.3 1.4 %shard_map.57.refs_2_ = f32[17,128,128]{2,1,0:T(8,128)S(1)} custom-call(s32[5,112]{1,0:T(8,128)S(1)} %get-tuple-element.22.order_ref, bf16[4,128,128]{2,1,0:T(8,128)(2,1)S(1)} %collective-permute-done.panel, bf16[96,128,128]{2,1,0:T(8,128)(2,1)S(1)} %get-tuple-element.24.blocks.refs_1_.refs_2_), custom_call_target="tpu_custom_call" | custom-call | flops 100663296 | bytes 786432 | tf_op jit(solution)/shard_map/pallas_call | solution.py:222
  10.7 0.8 %collective-permute-done.2.refs_0_ = bf16[4,128,128]{2,1,0:T(8,128)(2,1)S(1)} collective-permute-done((bf16[4,128,128]{2,1,0:T(8,128)(2,1)S(1)}, bf16[4,128,128]{2,1,0:T(8,128)(2,1)S(1)}, u32[]{:S(2)}, u32[]{:S(2)}) %collective-permute-start.2) | collective-permute-done | bytes 131104 | tf_op jit(solution)/shard_map/ppermute | solution.py:212
  11.5 0.0 collective-permute-start.3
  11.5 0.5 %collective-permute-start.1 = (bf16[4,128,128]{2,1,0:T(8,128)(2,1)S(1)}, bf16[4,128,128]{2,1,0:T(8,128)(2,1)S(1)}, u32[]{:S(2)}, u32[]{:S(2)}) collective-permute-start(bf16[4,128,128]{2,1,0:T(8,128)(2,1)S(1)} %collective-permute-done.panel), channel_id=1, source_target_pairs={{0,1},{1,0},{2,3},{3,2},{4,5},{5,4},{6,7},{7,6},{8,9},{9,8},{10,11... | collective-permute-start | bytes 393224 | tf_op jit(solution)/shard_map/ppermute | solution.py:215
  12.0 0.6 %shard_map.58.refs_3_ = f32[17,128,128]{2,1,0:T(8,128)S(1)} custom-call(s32[5,112]{1,0:T(8,128)S(1)} %get-tuple-element.22.order_ref, bf16[4,128,128]{2,1,0:T(8,128)(2,1)S(1)} %collective-permute-done.2.refs_0_, bf16[96,128,128]{2,1,0:T(8,128)(2,1)S(1)} %get-tuple-element.24.blocks.refs_1_.refs_2_, ...), custom_call_target="tpu_custom_call", output_to_operand_aliasing={{}: (3, {})} | custom-call | flops 100663296 | bytes 786432 | tf_op jit(solution)/shard_map/pallas_call | solution.py:232
  12.6 0.2 collective-permute-done.3.refs_1_
  12.8 0.2 collective-permute-done.1.refs_0_
  13.0 1.1 %shard_map.59 = (bf16[1,4,128,128]{3,2,1,0:T(8,128)(2,1)S(1)}, f32[17,128,128]{2,1,0:T(8,128)S(1)}) custom-call(s32[5,112]{1,0:T(8,128)S(1)} %get-tuple-element.22.order_ref, bf16[4,128,128]{2,1,0:T(8,128)(2,1)S(1)} %collective-permute-done.1.refs_0_, bf16[4,128,128]{2,1,0:T(8,128)(2,1)S(1)} %collective-permute-done.3.refs_1_, ...), custom_call_target="tpu_custom_call", output_to_operand_aliasing={{1}: (4, {})} | custom-call | flops 50331648 | bytes 393216 | tf_op jit(solution)/shard_map/pallas_call | solution.py:247
  14.1 1.6 %collective-permute-start.4 = (bf16[1,4,128,128]{3,2,1,0:T(8,128)(2,1)S(1)}, bf16[1,4,128,128]{3,2,1,0:T(8,128)(2,1)S(1)}, u32[]{:S(2)}, u32[]{:S(2)}) collective-permute-start(bf16[1,4,128,128]{3,2,1,0:T(8,128)(2,1)S(1)} %get-tuple-element.34), channel_id=1, source_target_pairs={{0,4},{4,0},{8,12},{12,8},{1,5},{5,1},{9,13},{13,9},{2,6},{6,2},{1... | collective-permute-start | bytes 393224 | tf_op jit(solution)/shard_map/ppermute | solution.py:215
  15.8 0.0 copy-start
  15.8 2.1 %shard_map.60 = (f32[4,128,128]{2,1,0:T(8,128)S(1)}, bf16[4,128,128]{2,1,0:T(8,128)(2,1)S(1)}, f32[1,4,128,128]{3,2,1,0:T(8,128)S(1)}) custom-call(s32[5,112]{1,0:T(8,128)S(1)} %get-tuple-element.22.order_ref, bf16[4,128,128]{2,1,0:T(8,128)(2,1)S(1)} %collective-permute-done.1.refs_0_, bf16[4,128,128]{2,1,0:T(8,128)(2,1)S(1)} %collective-permute-done.3.refs_1_, ...), custom_call_target="tpu_custom_call" | custom-call | flops 201326592 | bytes 1572864 | tf_op jit(solution)/shard_map/pallas_call | solution.py:262
  17.9 2.6 %collective-permute-done.4 = bf16[1,4,128,128]{3,2,1,0:T(8,128)(2,1)S(1)} collective-permute-done((bf16[1,4,128,128]{3,2,1,0:T(8,128)(2,1)S(1)}, bf16[1,4,128,128]{3,2,1,0:T(8,128)(2,1)S(1)}, u32[]{:S(2)}, u32[]{:S(2)}) %collective-permute-start.4) | collective-permute-done | bytes 131104 | tf_op jit(solution)/shard_map/ppermute | solution.py:215
  20.5 2.8 %collective-permute-start.5 = (bf16[4,128,128]{2,1,0:T(8,128)(2,1)S(1)}, bf16[4,128,128]{2,1,0:T(8,128)(2,1)S(1)}, u32[]{:S(2)}, u32[]{:S(2)}) collective-permute-start(bf16[4,128,128]{2,1,0:T(8,128)(2,1)S(1)} %fusion.1), channel_id=1, source_target_pairs={{0,8},{4,12},{8,0},{12,4},{1,9},{5,13},{9,1},{13,5},{2,10},{6,14},... | collective-permute-start | bytes 393224 | tf_op jit(solution)/shard_map/ppermute | solution.py:215
  23.3 1.4 %collective-permute-start.6 = (bf16[4,128,128]{2,1,0:T(8,128)(2,1)S(1)}, bf16[4,128,128]{2,1,0:T(8,128)(2,1)S(1)}, u32[]{:S(2)}, u32[]{:S(2)}) collective-permute-start(bf16[4,128,128]{2,1,0:T(8,128)(2,1)S(1)} %get-tuple-element.36), channel_id=1, source_target_pairs={{0,4},{4,0},{8,12},{12,8},{1,5},{5,1},{9,13},{13,9},{2,6},{6,2},{1... | collective-permute-start | bytes 393224 | tf_op jit(solution)/shard_map/ppermute | solution.py:215
  24.7 0.0 copy-done
  24.7 5.2 %collective-permute-done.5 = bf16[4,128,128]{2,1,0:T(8,128)(2,1)S(1)} collective-permute-done((bf16[4,128,128]{2,1,0:T(8,128)(2,1)S(1)}, bf16[4,128,128]{2,1,0:T(8,128)(2,1)S(1)}, u32[]{:S(2)}, u32[]{:S(2)}) %collective-permute-start.5) | collective-permute-done | bytes 131104 | tf_op jit(solution)/shard_map/ppermute | solution.py:215
  29.9 0.3 collective-permute-done.6
  30.2 0.8 %fusion = bf16[1,512,128]{2,1,0:T(8,128)(2,1)} fusion(f32[512]{0:T(512)S(1)} %bitcast.16, f32[1,512,128]{2,1,0:T(8,128)S(1)} %bitcast.14), kind=kLoop, calls=%fused_computation.1 | loop fusion | flops 131072 | bytes 395264 | tf_op jit(solution)/shard_map/convert_element_type | solution.py:282
  (3 shorter events, 0.1 us)
Async XLA Ops:
  1.0 8.3 %collective-permute-start = (bf16[4,128,128]{2,1,0:T(8,128)(2,1)S(1)}, bf16[4,128,128]{2,1,0:T(8,128)(2,1)S(1)}, u32[]{:S(2)}, u32[]{:S(2)}) collective-permute-start(bf16[4,128,128]{2,1,0:T(8,128)(2,1)S(1)} %shard_map.55), channel_id=1, source_target_pairs={{0,16},{1,17},{2,18},{3,19},{16,0},{17,1},{18,2},{19,3},{4,20},{5,... | collective-permute-start | bytes 393224 | tf_op jit(solution)/shard_map/ppermute | solution.py:212
  4.0 7.5 %collective-permute-start.2 = (bf16[4,128,128]{2,1,0:T(8,128)(2,1)S(1)}, bf16[4,128,128]{2,1,0:T(8,128)(2,1)S(1)}, u32[]{:S(2)}, u32[]{:S(2)}) collective-permute-start(bf16[4,128,128]{2,1,0:T(8,128)(2,1)S(1)} %shard_map.55), channel_id=1, source_target_pairs={{0,18},{1,19},{2,16},{3,17},{16,2},{17,3},{18,0},{19,1},{4,22},{5,... | collective-permute-start | bytes 393224 | tf_op jit(solution)/shard_map/ppermute | solution.py:212
  11.5 1.3 %collective-permute-start.3 = (bf16[4,128,128]{2,1,0:T(8,128)(2,1)S(1)}, bf16[4,128,128]{2,1,0:T(8,128)(2,1)S(1)}, u32[]{:S(2)}, u32[]{:S(2)}) collective-permute-start(bf16[4,128,128]{2,1,0:T(8,128)(2,1)S(1)} %collective-permute-done.2.refs_0_), channel_id=1, source_target_pairs={{0,1},{1,0},{2,3},{3,2},{4,5},{5,4},{6,7},{7,6},{8,9},{9,8},{10,11... | collective-permute-start | bytes 393224 | tf_op jit(solution)/shard_map/ppermute | solution.py:215
  11.5 1.5 %collective-permute-start.1 = (bf16[4,128,128]{2,1,0:T(8,128)(2,1)S(1)}, bf16[4,128,128]{2,1,0:T(8,128)(2,1)S(1)}, u32[]{:S(2)}, u32[]{:S(2)}) collective-permute-start(bf16[4,128,128]{2,1,0:T(8,128)(2,1)S(1)} %collective-permute-done.panel), channel_id=1, source_target_pairs={{0,1},{1,0},{2,3},{3,2},{4,5},{5,4},{6,7},{7,6},{8,9},{9,8},{10,11... | collective-permute-start | bytes 393224 | tf_op jit(solution)/shard_map/ppermute | solution.py:215
  14.1 6.3 %collective-permute-start.4 = (bf16[1,4,128,128]{3,2,1,0:T(8,128)(2,1)S(1)}, bf16[1,4,128,128]{3,2,1,0:T(8,128)(2,1)S(1)}, u32[]{:S(2)}, u32[]{:S(2)}) collective-permute-start(bf16[1,4,128,128]{3,2,1,0:T(8,128)(2,1)S(1)} %get-tuple-element.34), channel_id=1, source_target_pairs={{0,4},{4,0},{8,12},{12,8},{1,5},{5,1},{9,13},{13,9},{2,6},{6,2},{1... | collective-permute-start | bytes 393224 | tf_op jit(solution)/shard_map/ppermute | solution.py:215
  15.8 9.0 %copy-start = (s32[1,512]{1,0:T(1,128)S(1)}, s32[1,512]{1,0:T(1,128)}, u32[]{:S(2)}) copy-start(s32[1,512]{1,0:T(1,128)} %degrees_hbm.1) | copy-start | bytes 6148
  20.5 9.4 %collective-permute-start.5 = (bf16[4,128,128]{2,1,0:T(8,128)(2,1)S(1)}, bf16[4,128,128]{2,1,0:T(8,128)(2,1)S(1)}, u32[]{:S(2)}, u32[]{:S(2)}) collective-permute-start(bf16[4,128,128]{2,1,0:T(8,128)(2,1)S(1)} %fusion.1), channel_id=1, source_target_pairs={{0,8},{4,12},{8,0},{12,4},{1,9},{5,13},{9,1},{13,5},{2,10},{6,14},... | collective-permute-start | bytes 393224 | tf_op jit(solution)/shard_map/ppermute | solution.py:215
  23.3 6.9 %collective-permute-start.6 = (bf16[4,128,128]{2,1,0:T(8,128)(2,1)S(1)}, bf16[4,128,128]{2,1,0:T(8,128)(2,1)S(1)}, u32[]{:S(2)}, u32[]{:S(2)}) collective-permute-start(bf16[4,128,128]{2,1,0:T(8,128)(2,1)S(1)} %get-tuple-element.36), channel_id=1, source_target_pairs={{0,4},{4,0},{8,12},{12,8},{1,5},{5,1},{9,13},{13,9},{2,6},{6,2},{1... | collective-permute-start | bytes 393224 | tf_op jit(solution)/shard_map/ppermute | solution.py:215
where the time goes:
time: 30.7 us; the launch traced here: 31 us
  starting transfers between devices  10.9 us (36%)
  Pallas kernels  9.9 us (32%)
  waiting for transfers between devices  9.2 us (30%)
  other arithmetic  0.95 us (3%)
    ppermute x5, waiting for transfers between devices, paired(): lax.ppermute(value, axis, [(at, at ^ hop) for at in range(lax.axis_size(a...  8.41 us
    ppermute x5, starting transfers between devices, paired(): lax.ppermute(value, axis, [(at, at ^ hop) for at in range(lax.axis_size(a...  6.42 us
    ppermute x2, starting transfers between devices, across(): return lax.ppermute(value, ('side', 'blk'), pairs)  4.49 us
    pallas_call x1, Pallas kernels, stage_blocks(): pl.pallas_call(functools.partial(stage_kernel, blks, groups, tiles_dev),...  3.75 us
    pallas_call x1, Pallas kernels, shards(): pl.pallas_call(functools.partial(near_kernel, tiles_dev, mine_chunks), ou...  2.08 us
    pallas_call x1, Pallas kernels, shards(): pl.pallas_call(first_kernel, out_shape=total_shape, in_specs=[SMEM] + [VM...  1.38 us
    pallas_call x1, Pallas kernels, shards(): pl.pallas_call(functools.partial(far_kernel, tiles_dev, far_chunks), out_...  1.11 us
    pallas_call x1, Pallas kernels, scale_rows(): pl.pallas_call(scale_kernel, out_shape=jax.ShapeDtypeStruct(codes.shape,...  0.97 us
  transfers between devices with their start and end apart: 7, of which 6 were waited for; matrix products, arithmetic and copies ran while one was open for 0% of the time, Pallas kernels for 25%

commit v1 on v0

--- a/solution.py
+++ b/solution.py
@@ -8,7 +8,7 @@
 from jax.sharding import PartitionSpec as P
 
 UNROLL = 8
-STAGES = 4
+STAGES = 3
 VMEM = pl.BlockSpec(memory_space=pltpu.VMEM)
 SMEM = pl.BlockSpec(memory_space=pltpu.SMEM)
 HBM = pl.BlockSpec(memory_space=pltpu.HBM)
@@ -75,7 +75,6 @@
     copy.start()
     fetch.wait()
     my_blk = place_ref[0]
-    my_grp = place_ref[1]
     capacity = index_ref.shape[1]
     source_tiles = blks * tiles_dev
 
@@ -85,11 +84,10 @@
         hop, row = split(origin, tiles_dev)
         chunk, tile = split(target, tiles_dev)
         hop = hop ^ my_blk
-        chunk = chunk ^ my_grp
-        near = jnp.where((chunk >= 2) & ((chunk & 1) == 1), 2, 3)
-        stage = jnp.where((hop & 1) == 1, near, jnp.where(hop == 0, 0, 1))
+        odd = hop & 1
+        stage = jnp.where(hop == 0, 0, 1 + odd)
         stage = jnp.where(origin < source_tiles, stage, STAGES)
-        panel = (hop >> 1) - (stage == 1).astype(jnp.int32)
+        panel = jnp.where(odd == 1, hop >> 1, jnp.maximum((hop >> 1) - 1, 0))
         word = pack(slot, panel * tiles_dev + row, chunk * tiles_dev + tile)
         where = jnp.int32(0)
         for at, position in enumerate(nexts):
@@ -165,22 +163,13 @@
     add_products(1, order_ref, blocks, source, total)
 
 
-def far_kernel(tiles_dev, chunks, order_ref, *refs):
-    *panels, blocks, _, far, total, source = refs
+def last_kernel(tiles_dev, place_ref, order_ref, *refs):
+    *panels, blocks, total, own, sent, source = refs
     gather_panels(panels, source)
     add_products(2, order_ref, blocks, source, total)
-    for at, chunk in enumerate(chunks):
-        far[at] = total[chunk * tiles_dev : (chunk + 1) * tiles_dev].astype(far.dtype)
-
-
-def near_kernel(tiles_dev, chunks, order_ref, *refs):
-    *panels, blocks, total, own, near, mine, source = refs
-    gather_panels(panels, source)
-    add_products(3, order_ref, blocks, source, total)
-    own[...] = total[:tiles_dev]
-    near[...] = total[tiles_dev : 2 * tiles_dev].astype(near.dtype)
-    for at, chunk in enumerate(chunks):
-        mine[at] = total[chunk * tiles_dev : (chunk + 1) * tiles_dev]
+    own[...] = total[pl.ds(place_ref[1] * tiles_dev, tiles_dev)]
+    for chunk in range(sent.shape[0]):
+        sent[chunk] = total[chunk * tiles_dev : (chunk + 1) * tiles_dev].astype(sent.dtype)
 
 
 def cost_of(slots, tile_rows, row_width):
@@ -243,41 +232,21 @@
     )(order, *diagonal, blocks, total)
     *others, total = lax.optimization_barrier((*others, total))
     others_scratch = [pltpu.VMEM((len(others) * tiles_dev, tile_rows, row_width), jnp.bfloat16)]
-    far_chunks = range(3, groups, 2)
-    far, total = pl.pallas_call(
-        functools.partial(far_kernel, tiles_dev, far_chunks),
-        out_shape=[
-            jax.ShapeDtypeStruct((len(far_chunks),) + part, jnp.bfloat16),
-            total_shape,
-        ],
-        in_specs=[SMEM] + [VMEM] * (len(others) + 2),
-        out_specs=[VMEM, VMEM],
-        input_output_aliases={len(others) + 2: 1},
-        scratch_shapes=others_scratch,
-        compiler_params=LIMIT,
-        cost_estimate=cost_of(capacity // 8, tile_rows, row_width),
-    )(order, *others, blocks, total)
-    far_arrived = paired(far, "grp", 1)
-    mine_chunks = range(2, groups, 2)
-    own, near, mine = pl.pallas_call(
-        functools.partial(near_kernel, tiles_dev, mine_chunks),
+    own, sent = pl.pallas_call(
+        functools.partial(last_kernel, tiles_dev),
         out_shape=[
             jax.ShapeDtypeStruct(part, jnp.float32),
-            jax.ShapeDtypeStruct(part, jnp.bfloat16),
-            jax.ShapeDtypeStruct((len(mine_chunks),) + part, jnp.float32),
-        ],
-        in_specs=[SMEM] + [VMEM] * (len(others) + 2),
-        out_specs=[VMEM] * 3,
+            jax.ShapeDtypeStruct((groups,) + part, jnp.bfloat16),
+        ],
+        in_specs=[SMEM, SMEM] + [VMEM] * (len(others) + 2),
+        out_specs=[VMEM] * 2,
         scratch_shapes=others_scratch,
         compiler_params=LIMIT,
         cost_estimate=cost_of(capacity // 2, tile_rows, row_width),
-    )(order, *others, blocks, total)
-    summed = own
-    for at, hop in enumerate(mine_chunks):
-        pair = (mine[at] + far_arrived[at].astype(jnp.float32)).astype(jnp.bfloat16)
-        near, pair = lax.optimization_barrier((near, pair))
-        summed = summed + paired(pair, "grp", hop).astype(jnp.float32)
-    summed = summed + paired(near, "grp", 1).astype(jnp.float32)
+    )(place, order, *others, blocks, total)
+    arrived = lax.all_to_all(sent, "grp", split_axis=0, concat_axis=0)
+    mine = jnp.arange(groups)[:, None, None, None] == lax.axis_index("grp")
+    summed = own + jnp.sum(jnp.where(mine, 0.0, arrived.astype(jnp.float32)), axis=0)
     inverse = lax.rsqrt(degrees.astype(jnp.float32))
     return (summed.reshape(1, row_count, row_width) * inverse[..., None]).astype(jnp.bfloat16)
 

time: 30.7 us -> 37.2 us (1.21)
  waiting for transfers between devices: 9.2 us -> 14.9 us
  starting transfers between devices: 10.9 us -> 11.5 us
    all_to_all x0 -> x1, waiting for transfers between devices: none -> 14.9 us  [shards(): arrived = lax.all_to_all(sent, 'grp', split_axis=0, concat_axis=0)]
    ppermute x5 -> x2, waiting for transfers between devices: 8.41 us -> 0.01 us  [paired(): lax.ppermute(value, axis, [(at, at ^ hop) for at in range(lax.axis_size(a...]
    all_to_all x0 -> x1, starting transfers between devices: none -> 6.41 us  [shards(): arrived = lax.all_to_all(sent, 'grp', split_axis=0, concat_axis=0)]
    ppermute x5 -> x2, starting transfers between devices: 6.42 us -> 0.57 us  [paired(): lax.ppermute(value, axis, [(at, at ^ hop) for at in range(lax.axis_size(a...]
    pallas_call x2 -> x1, Pallas kernels: 3.19 us -> 1.93 us  [shards(): pl.pallas_call(functools.partial(last_kernel, tiles_dev), out_shape=[jax....]
    pallas_call x1, Pallas kernels: 1.38 us -> 2.59 us  [shards(): pl.pallas_call(first_kernel, out_shape=total_shape, in_specs=[SMEM] + [VM...]
    ppermute x2, waiting for transfers between devices: 0.79 us -> 0.01 us  [across(): return lax.ppermute(value, ('side', 'blk'), pairs)]
    pallas_call x1, Pallas kernels: 0.61 us -> 1.05 us  [shards(): pl.pallas_call(second_kernel, out_shape=total_shape, in_specs=[SMEM] + [V...]
  transfers between devices with their start and end apart: 7 -> 5, of which waited for: 6 -> 1; matrix products, arithmetic and copies ran while one was open for 0% -> 0% of each run, Pallas kernels for 25% -> 19%
where the time goes in v1:
time: 37.2 us; the launch traced here: 37.5 us
  waiting for transfers between devices  14.9 us (40%)
  starting transfers between devices  11.5 us (31%)
  Pallas kernels  9.94 us (27%)
  other arithmetic  1.11 us (3%)
    all_to_all x1, waiting for transfers between devices, shards(): arrived = lax.all_to_all(sent, 'grp', split_axis=0, concat_axis=0)  14.9 us
    all_to_all x1, starting transfers between devices, shards(): arrived = lax.all_to_all(sent, 'grp', split_axis=0, concat_axis=0)  6.41 us
    ppermute x2, starting transfers between devices, across(): return lax.ppermute(value, ('side', 'blk'), pairs)  4.49 us
    pallas_call x1, Pallas kernels, stage_blocks(): pl.pallas_call(functools.partial(stage_kernel, blks, groups, tiles_dev),...  3.41 us
    pallas_call x1, Pallas kernels, shards(): pl.pallas_call(first_kernel, out_shape=total_shape, in_specs=[SMEM] + [VM...  2.59 us
    pallas_call x1, Pallas kernels, shards(): pl.pallas_call(functools.partial(last_kernel, tiles_dev), out_shape=[jax....  1.93 us
    pallas_call x1, Pallas kernels, shards(): pl.pallas_call(second_kernel, out_shape=total_shape, in_specs=[SMEM] + [V...  1.05 us
    pallas_call x1, Pallas kernels, scale_rows(): pl.pallas_call(scale_kernel, out_shape=jax.ShapeDtypeStruct(codes.shape,...  0.97 us
  transfers between devices with their start and end apart: 5, of which 1 were waited for; matrix products, arithmetic and copies ran while one was open for 0% of the time, Pallas kernels for 19%

profile of v1, /device:TPU:0, one launch (start us, length us, event | category | flops | bytes accessed | tf_op | source)
XLA Modules:
  0.0 37.5 jit_solution(16785159244415669003)
XLA Ops:
  0.0 1.0 %shard_map.55 = bf16[4,128,128]{2,1,0:T(8,128)(2,1)S(1)} custom-call(s32[1,4]{1,0:T(1,128)} %exps_hbm.1, s32[1,512]{1,0:T(1,128)} %degrees_hbm.1, bf16[4,128,128]{2,1,0:T(8,128)(2,1)} %bitcast.13), custom_call_target="tpu_custom_call" | custom-call | flops 65536 | bytes 262144 | tf_op jit(solution)/shard_map/pallas_call | solution.py:51
  1.0 3.0 %collective-permute-start = (bf16[4,128,128]{2,1,0:T(8,128)(2,1)S(1)}, bf16[4,128,128]{2,1,0:T(8,128)(2,1)S(1)}, u32[]{:S(2)}, u32[]{:S(2)}) collective-permute-start(bf16[4,128,128]{2,1,0:T(8,128)(2,1)S(1)} %shard_map.55), channel_id=1, source_target_pairs={{0,16},{1,17},{2,18},{3,19},{16,0},{17,1},{18,2},{19,3},{4,20},{5,... | collective-permute-start | bytes 393224 | tf_op jit(solution)/shard_map/ppermute | solution.py:201
  4.0 1.5 %collective-permute-start.2 = (bf16[4,128,128]{2,1,0:T(8,128)(2,1)S(1)}, bf16[4,128,128]{2,1,0:T(8,128)(2,1)S(1)}, u32[]{:S(2)}, u32[]{:S(2)}) collective-permute-start(bf16[4,128,128]{2,1,0:T(8,128)(2,1)S(1)} %shard_map.55), channel_id=1, source_target_pairs={{0,18},{1,19},{2,16},{3,17},{16,2},{17,3},{18,0},{19,1},{4,22},{5,... | collective-permute-start | bytes 393224 | tf_op jit(solution)/shard_map/ppermute | solution.py:201
  5.5 0.1 pad_add_fusion.place_ref
  5.5 3.4 %shard_map.56 = (s32[4,112]{1,0:T(4,128)S(1)}, bf16[96,128,128]{2,1,0:T(8,128)(2,1)S(1)}) custom-call(s32[2]{0:T(128)S(1)} %pad_add_fusion.place_ref, s32[2,96]{1,0:T(2,128)} %bitcast.15, bf16[96,128,128]{2,1,0:T(8,128)(2,1)} %bitcast.11), custom_call_target="tpu_custom_call" | custom-call | tf_op jit(solution)/shard_map/pallas_call | solution.py:120
  9.0 0.0 collective-permute-done.panel
  9.0 2.6 %shard_map.57.refs_2_ = f32[17,128,128]{2,1,0:T(8,128)S(1)} custom-call(s32[4,112]{1,0:T(4,128)S(1)} %get-tuple-element.17.order_ref, bf16[4,128,128]{2,1,0:T(8,128)(2,1)S(1)} %collective-permute-done.panel, bf16[96,128,128]{2,1,0:T(8,128)(2,1)S(1)} %get-tuple-element.19.blocks.refs_1_.refs_2_), custom_call_target="tpu_custom_call" | custom-call | flops 100663296 | bytes 786432 | tf_op jit(solution)/shard_map/pallas_call | solution.py:211
  11.6 0.0 collective-permute-done.2.refs_0_
  11.6 0.1 collective-permute-start.3
  11.7 0.5 %collective-permute-start.1 = (bf16[4,128,128]{2,1,0:T(8,128)(2,1)S(1)}, bf16[4,128,128]{2,1,0:T(8,128)(2,1)S(1)}, u32[]{:S(2)}, u32[]{:S(2)}) collective-permute-start(bf16[4,128,128]{2,1,0:T(8,128)(2,1)S(1)} %collective-permute-done.panel), channel_id=1, source_target_pairs={{0,1},{1,0},{2,3},{3,2},{4,5},{5,4},{6,7},{7,6},{8,9},{9,8},{10,11... | collective-permute-start | bytes 393224 | tf_op jit(solution)/shard_map/ppermute | solution.py:204
  12.2 1.0 %shard_map.58.refs_3_ = f32[17,128,128]{2,1,0:T(8,128)S(1)} custom-call(s32[4,112]{1,0:T(4,128)S(1)} %get-tuple-element.17.order_ref, bf16[4,128,128]{2,1,0:T(8,128)(2,1)S(1)} %collective-permute-done.2.refs_0_, bf16[96,128,128]{2,1,0:T(8,128)(2,1)S(1)} %get-tuple-element.19.blocks.refs_1_.refs_2_, ...), custom_call_target="tpu_custom_call", output_to_operand_aliasing={{}: (3, {})} | custom-call | flops 100663296 | bytes 786432 | tf_op jit(solution)/shard_map/pallas_call | solution.py:221
  13.2 0.0 copy-start
  13.2 0.0 collective-permute-done.3.refs_1_
  13.2 0.0 collective-permute-done.1.refs_0_
  13.2 1.9 %shard_map.59 = (f32[4,128,128]{2,1,0:T(8,128)S(1)}, bf16[4,4,128,128]{3,2,1,0:T(8,128)(2,1)}) custom-call(s32[2]{0:T(128)S(1)} %pad_add_fusion.place_ref, s32[4,112]{1,0:T(4,128)S(1)} %get-tuple-element.17.order_ref, bf16[4,128,128]{2,1,0:T(8,128)(2,1)S(1)} %collective-permute-done.1.refs_0_, bf16[4,128,128]{2,1,0:T(8,128)(2,1)S(1)} %collective-permute-done.3.refs_1_, ...), custom_call_target="tpu_custom_call" | custom-call | flops 201326592 | bytes 1572864 | tf_op jit(solution)/shard_map/pallas_call | solution.py:235
  15.2 6.4 %all-to-all-start = ((bf16[4,4,128,128]{3,2,1,0:T(8,128)(2,1)}), bf16[4,4,128,128]{3,2,1,0:T(8,128)(2,1)S(1)}, u32[]{:S(2)}, u32[]{:S(2)}) async-start(bf16[4,4,128,128]{3,2,1,0:T(8,128)(2,1)} %get-tuple-element.26), calls=%async_computation | async-start | bytes 1048576 | tf_op jit(solution)/shard_map/all_to_all | solution.py:247
  21.6 0.0 copy-done
  21.6 14.9 %all-to-all-done = bf16[4,4,128,128]{3,2,1,0:T(8,128)(2,1)S(1)} async-done(((bf16[4,4,128,128]{3,2,1,0:T(8,128)(2,1)}), bf16[4,4,128,128]{3,2,1,0:T(8,128)(2,1)S(1)}, u32[]{:S(2)}, u32[]{:S(2)}) %all-to-all-start) | async-done | bytes 524320 | tf_op jit(solution)/shard_map/all_to_all | solution.py:247
  36.5 0.2 select_reduce_fusion
  36.7 0.8 %fusion = bf16[1,512,128]{2,1,0:T(8,128)(2,1)} fusion(f32[512]{0:T(512)S(1)} %bitcast.14, f32[1,512,128]{2,1,0:T(8,128)S(1)} %bitcast.12), kind=kLoop, calls=%fused_computation.2 | loop fusion | flops 131072 | bytes 395264 | tf_op jit(solution)/shard_map/convert_element_type | solution.py:251
  (3 shorter events, 0.1 us)
Async XLA Ops:
  1.0 8.0 %collective-permute-start = (bf16[4,128,128]{2,1,0:T(8,128)(2,1)S(1)}, bf16[4,128,128]{2,1,0:T(8,128)(2,1)S(1)}, u32[]{:S(2)}, u32[]{:S(2)}) collective-permute-start(bf16[4,128,128]{2,1,0:T(8,128)(2,1)S(1)} %shard_map.55), channel_id=1, source_target_pairs={{0,16},{1,17},{2,18},{3,19},{16,0},{17,1},{18,2},{19,3},{4,20},{5,... | collective-permute-start | bytes 393224 | tf_op jit(solution)/shard_map/ppermute | solution.py:201
  4.0 7.6 %collective-permute-start.2 = (bf16[4,128,128]{2,1,0:T(8,128)(2,1)S(1)}, bf16[4,128,128]{2,1,0:T(8,128)(2,1)S(1)}, u32[]{:S(2)}, u32[]{:S(2)}) collective-permute-start(bf16[4,128,128]{2,1,0:T(8,128)(2,1)S(1)} %shard_map.55), channel_id=1, source_target_pairs={{0,18},{1,19},{2,16},{3,17},{16,2},{17,3},{18,0},{19,1},{4,22},{5,... | collective-permute-start | bytes 393224 | tf_op jit(solution)/shard_map/ppermute | solution.py:201
  11.6 1.6 %collective-permute-start.3 = (bf16[4,128,128]{2,1,0:T(8,128)(2,1)S(1)}, bf16[4,128,128]{2,1,0:T(8,128)(2,1)S(1)}, u32[]{:S(2)}, u32[]{:S(2)}) collective-permute-start(bf16[4,128,128]{2,1,0:T(8,128)(2,1)S(1)} %collective-permute-done.2.refs_0_), channel_id=1, source_target_pairs={{0,1},{1,0},{2,3},{3,2},{4,5},{5,4},{6,7},{7,6},{8,9},{9,8},{10,11... | collective-permute-start | bytes 393224 | tf_op jit(solution)/shard_map/ppermute | solution.py:204
  11.7 1.6 %collective-permute-start.1 = (bf16[4,128,128]{2,1,0:T(8,128)(2,1)S(1)}, bf16[4,128,128]{2,1,0:T(8,128)(2,1)S(1)}, u32[]{:S(2)}, u32[]{:S(2)}) collective-permute-start(bf16[4,128,128]{2,1,0:T(8,128)(2,1)S(1)} %collective-permute-done.panel), channel_id=1, source_target_pairs={{0,1},{1,0},{2,3},{3,2},{4,5},{5,4},{6,7},{7,6},{8,9},{9,8},{10,11... | collective-permute-start | bytes 393224 | tf_op jit(solution)/shard_map/ppermute | solution.py:204
  13.2 8.4 %copy-start = (s32[1,512]{1,0:T(1,128)S(1)}, s32[1,512]{1,0:T(1,128)}, u32[]{:S(2)}) copy-start(s32[1,512]{1,0:T(1,128)} %degrees_hbm.1) | copy-start | bytes 6148
  15.2 21.3 %all-to-all-start = ((bf16[4,4,128,128]{3,2,1,0:T(8,128)(2,1)}), bf16[4,4,128,128]{3,2,1,0:T(8,128)(2,1)S(1)}, u32[]{:S(2)}, u32[]{:S(2)}) async-start(bf16[4,4,128,128]{3,2,1,0:T(8,128)(2,1)} %get-tuple-element.26), calls=%async_computation | async-start | bytes 1048576 | tf_op jit(solution)/shard_map/all_to_all | solution.py:247
